TPU v7x, 32 devices: a whole 2x2x4 slice. The times are simulated.
32 devices in a mesh: aux: 4 (over y, core), virt: 8 (over z, x).
Axes of the slice: x: 2, y: 2, z: 4, core: 2. Of those that a mesh axis runs over, the one named last changes fastest.
Arguments:
- integrals: float32 [1024, 6, 2560], P('virt', None, 'aux'), may hold values from -1.25 to 1.25
- metric_root: float32 [2560, 2560], P(None, 'aux'), may hold values from -0.125 to 0.125
- occ_energy: float32 [256], replicated, may hold values from -1.5 to -0.3
- virt_energy: float32 [1024], replicated, may hold values from 0.2 to 3
- batch_index: int32 [6], replicated, may hold values from 0 to 255, as said below
- virt_order: int32 [1024], replicated, may hold values from 0 to 1023, each once
Outputs:
- density: float32 [1024, 6, 2560], P('virt', None, 'aux')
Inputs may be any that keep to these rules, and one draw needn't show every extreme that they name: `batch_index`: 6 distinct occupied orbital numbers, among them 0 and 255. `virt_order`: each number appears once.
All inputs are finite; a program needn't handle non-finite values.
Results may differ from a plain program's by a relative error of at most 0.000057.
Values sent between devices are 32-bit elements; how exact they have to be, the bound alone decides.
A program may use at most 192 MiB of HBM per device.

v0:
```python
import jax
import jax.numpy as jnp
from jax import lax
from jax.sharding import PartitionSpec as P

precise = lax.Precision.HIGHEST


def from_root(block, axis, holder):
    block = jnp.where(lax.axis_index(axis) == holder, block, jnp.zeros_like(block))
    return lax.psum(block, axis)


def select_levels(levels_table, picked):
    places = jnp.arange(levels_table.shape[0], dtype=jnp.int32)
    return jnp.sum(
        jnp.where(picked[:, None] == places[None, :], levels_table[None, :], 0.0), axis=1
    )


def pair_density(left_rows, right_rows, row_levels, col_levels, occ_levels):
    row_count = row_levels.shape[0]
    col_count = col_levels.shape[0]
    occ_count = occ_levels.shape[0]
    pair_ints = lax.dot_general(
        left_rows,
        right_rows,
        (((1,), (1,)), ((), ())),
        precision=precise,
        preferred_element_type=jnp.float32,
    )
    pair_ints = pair_ints.reshape(row_count, occ_count, col_count, occ_count)
    swapped = pair_ints.transpose(0, 3, 2, 1)
    denominator = (
        occ_levels[None, :, None, None]
        + occ_levels[None, None, None, :]
        - row_levels[:, None, None, None]
        - col_levels[None, None, :, None]
    )
    weighted = ((2.0 * pair_ints - swapped) / denominator).reshape(
        row_count * occ_count, col_count * occ_count
    )
    return jnp.dot(weighted, right_rows, precision=precise, preferred_element_type=jnp.float32)


def shards(integrals, metric_root, occ_energy, virt_energy, batch_index, virt_order):
    virt_local, batch_count, aux_local = integrals.shape
    aux_total = metric_root.shape[0]
    virt_total = virt_order.shape[0]
    aux_count = lax.axis_size("aux")
    virt_count = lax.axis_size("virt")
    aux_place = lax.axis_index("aux")
    virt_place = lax.axis_index("virt")
    occ_levels = select_levels(occ_energy, batch_index)
    partial_term = lax.dot_general(
        integrals.reshape(virt_local * batch_count, aux_local),
        metric_root,
        (((1,), (1,)), ((), ())),
        precision=precise,
        preferred_element_type=jnp.float32,
    )
    panel_rows = lax.psum(partial_term, "aux")
    row_order = lax.dynamic_slice_in_dim(virt_order, virt_place * virt_local, virt_local, 0)
    row_levels = select_levels(virt_energy, row_order)
    block_width = virt_total // aux_count
    owners_each = virt_count // aux_count
    panels = []
    for owner in range(owners_each):
        panels.append(from_root(panel_rows, "virt", aux_place * owners_each + owner))
    panel_cols = jnp.concatenate(panels, axis=0)
    col_order = lax.dynamic_slice_in_dim(virt_order, aux_place * block_width, block_width, 0)
    col_levels = select_levels(virt_energy, col_order)
    partial_density = pair_density(panel_rows, panel_cols, row_levels, col_levels, occ_levels)
    result = lax.psum_scatter(
        partial_density.reshape(virt_local, batch_count, aux_total),
        "aux",
        scatter_dimension=2,
        tiled=True,
    )
    return result


def solution(mesh):
    return jax.shard_map(
        shards,
        mesh=mesh,
        in_specs=(P("virt", None, "aux"), P(None, "aux"), P(), P(), P(), P()),
        out_specs=P("virt", None, "aux"),
        check_vma=False,
    )
```

profile of v0, /device:TPU:0, one launch (start us, length us, event | category | flops | bytes accessed | tf_op | source)
XLA Modules:
  0.0 1091.8 jit_solution(6668368526564748358)
XLA Ops:
  6.5 0.0 all-reduce.4.cloned.1.call-start
  6.5 2.7 copy.17
  9.3 1.4 reshape.54
  10.7 23.4 %fusion.3 = f32[768,2560]{1,0:T(8,128)} fusion(f32[768,640]{1,0:T(8,128)} %reshape.54, f32[2560,640]{1,0:T(8,128)} %param.7), kind=kOutput, calls=%fused_computation.16 | convolution fusion | flops 15099494400 | bytes 16384000 | tf_op jit(solution)/shard_map/dot_general | solution.py:55
  34.1 0.0 all-reduce.4.cloned.1.call-update
  34.2 0.0 all-reduce.6.cloned.1.call-start
  34.2 147.9 %all-reduce.4.cloned.1.call-done = f32[768,2560]{1,0:T(8,128)} async-done(((f32[768,2560]{1,0:T(8,128)}), f32[768,2560]{1,0:T(8,128)}) %all-reduce.4.cloned.1.call-update) | async-done | bytes 7864336 | tf_op jit(solution)/shard_map/psum | solution.py:62
  182.1 10.8 broadcast_select_fusion
  193.0 0.0 all-reduce.6.cloned.1.call-update
  193.0 0.0 reduce-scatter.2.cloned.1.call-start
  193.1 0.8 dynamic_slice.6
  193.8 0.8 dynamic_slice.7
  194.6 0.0 copy-done.3
  194.6 0.2 select_reduce_fusion.2
  194.8 0.2 select_reduce_fusion.1
  195.0 0.3 select_reduce_fusion
  195.2 0.1 broadcast_add_fusion
  195.3 0.1 broadcast_subtract_fusion
  195.4 479.9 %all-reduce.6.cloned.1.call-done = (f32[768,2560]{1,0:T(8,128)}, f32[768,2560]{1,0:T(8,128)}) async-done(((f32[768,2560]{1,0:T(8,128)}, f32[768,2560]{1,0:T(8,128)}), (f32[768,2560]{1,0:T(8,128)}, f32[768,2560]{1,0:T(8,128)})) %all-reduce.6.cloned.1.call-update) | async-done | bytes 15728656 | tf_op jit(solution)/shard_map/psum | solution.py:11
  675.3 3.8 constant_dynamic-update-slice_fusion.1
  679.0 3.8 constant_dynamic-update-slice_fusion
  682.8 5.5 copy-done
  688.3 43.9 %fusion.4 = f32[768,1536]{1,0:T(8,128)} fusion(f32[768,2560]{1,0:T(8,128)} %all-reduce.4.cloned.1.call-done, f32[1536,2560]{1,0:T(8,128)S(1)} %constant_dynamic-update-slice_fusion), kind=kOutput, calls=%fused_computation.17 | convolution fusion | flops 36238786560 | bytes 28311552 | tf_op jit(solution)/shard_map/dot_general | solution.py:25
  732.2 105.9 %reshape.55 = f32[128,6,256,6]{3,2,1,0:T(8,128)} reshape(f32[768,1536]{1,0:T(8,128)} %fusion.4) | data formatting | bytes 9437184 | tf_op jit(solution)/shard_map/reshape | solution.py:32
  838.2 59.0 %copy.18 = f32[128,6,256,6]{2,0,3,1:T(8,128)} copy(f32[128,6,256,6]{3,2,1,0:T(8,128)} %reshape.55) | data formatting | bytes 9437184 | tf_op jit(solution)/shard_map/reshape | solution.py:32
  897.2 59.0 %copy.19 = f32[128,6,256,6]{2,0,1,3:T(8,128)} copy(f32[128,6,256,6]{3,2,1,0:T(8,128)} %reshape.55) | data formatting | bytes 9437184 | tf_op jit(solution)/shard_map/reshape | solution.py:32
  956.2 5.7 fusion.2
  961.9 6.2 copy.20
  968.1 6.6 dot_general.13
  974.7 42.2 %fusion = f32[128,6,2560]{2,0,1:T(8,128)} fusion(f32[128,6,1536]{0,2,1:T(8,128)} %dot_general.13, f32[1536,2560]{1,0:T(8,128)} %copy-done), kind=kOutput, calls=%fused_computation | convolution fusion | flops 36238786560 | bytes 28311552 | tf_op jit(solution)/shard_map/dot_general | solution.py:43
  1016.9 0.0 reduce-scatter.2.cloned.1.call-update
  1016.9 68.2 %reduce-scatter.2.cloned.1.call-done = f32[128,6,640]{2,0,1:T(8,128)} async-done(((f32[128,6,2560]{2,0,1:T(8,128)}), f32[128,6,640]{2,0,1:T(8,128)}) %reduce-scatter.2.cloned.1.call-update) | async-done | bytes 1966096 | tf_op jit(solution)/shard_map/reduce_scatter | solution.py:74
  (6 shorter events, 0.0 us)
Async XLA Ops:
  6.5 175.6 %all-reduce.4.cloned.1.call-start = ((), (), s32[]{:S(2)}) async-start(), calls=%async_computation.1 | async-start | bytes 15728640 | tf_op jit(solution)/shard_map/psum | solution.py:62
  34.2 641.1 %all-reduce.6.cloned.1.call-start = ((), (), s32[]{:S(2)}) async-start(), calls=%async_computation.3 | async-start | bytes 31457280 | tf_op jit(solution)/shard_map/psum | solution.py:11
  193.0 1.6 copy-start.2
  193.0 1.6 copy-start.3
  193.0 1.8 copy-start.1
  193.0 892.1 %reduce-scatter.2.cloned.1.call-start = ((), (), s32[]{:S(2)}) async-start(), calls=%async_computation.2 | async-start | bytes 9830400 | tf_op jit(solution)/shard_map/reduce_scatter | solution.py:74
  682.8 5.5 copy-start
Sparse Core Ops, SparseCore 0:
  34.3 147.8 all-reduce.3
  193.1 482.0 all-reduce.5
  1017.0 68.0 reduce-scatter.1
where the time goes:
time: 1110 us; the launch traced here: 1090 us
  waiting for transfers between devices  696 us (63%)
  local copies, waits for them, and re-layouts  256 us (23%)
  matrix products  110 us (10%)
  other arithmetic  17.3 us (2%)
  between operations  13.4 us (1%)
    psum x1, waiting for transfers between devices, from_root(): return lax.psum(block, axis)  480 us
    reshape x3, local copies, waits for them, and re-layouts, pair_density(): pair_ints = pair_ints.reshape(row_count, occ_count, col_count, occ_count)  224 us
    psum x1, waiting for transfers between devices, shards(): panel_rows = lax.psum(partial_term, 'aux')  148 us
    reduce_scatter x1, waiting for transfers between devices, shards(): lax.psum_scatter(partial_density.reshape(virt_local, batch_count, aux_tot...  68.2 us
    dot_general x1, matrix products, pair_density(): lax.dot_general(left_rows, right_rows, (((1,), (1,)), ((), ())), precisio...  43.9 us
    dot_general x1, matrix products, pair_density(): jnp.dot(weighted, right_rows, precision=precise, preferred_element_type=j...  42.2 us
    dot_general x1, matrix products, shards(): lax.dot_general(integrals.reshape(virt_local * batch_count, aux_local), m...  23.4 us
  transfers between devices with their start and end apart: 3, of which 3 were waited for; matrix products, arithmetic and copies ran while one was open for 0% of the time, Pallas kernels for 0%

commit v1 on v0

v1 whole, which is shorter than its diff:
```python
import jax
import jax.numpy as jnp
from jax import lax
from jax.sharding import PartitionSpec as P

precise = lax.Precision.HIGH


def select_levels(levels_table, picked):
    places = jnp.arange(levels_table.shape[0], dtype=jnp.int32)
    return jnp.sum(
        jnp.where(picked[:, None] == places[None, :], levels_table[None, :], 0.0), axis=1
    )


def shards(integrals, metric_root, occ_energy, virt_energy, batch_index, virt_order):
    virt_local, batch_count, aux_local = integrals.shape
    aux_total = metric_root.shape[0]
    aux_count = lax.axis_size("aux")
    virt_count = lax.axis_size("virt")
    aux_place = lax.axis_index("aux")
    virt_place = lax.axis_index("virt")
    share = virt_local // aux_count
    occ_levels = select_levels(occ_energy, batch_index)
    virt_levels = select_levels(virt_energy, virt_order)
    row_levels = lax.dynamic_slice_in_dim(virt_levels, virt_place * virt_local, virt_local, 0)
    col_levels = lax.dynamic_slice_in_dim(
        virt_levels.reshape(virt_count, aux_count, share), aux_place, 1, 1
    ).reshape(virt_count * share)

    by_occ = integrals.transpose(1, 0, 2).reshape(batch_count * virt_local, aux_local)
    partial_term = lax.dot_general(
        by_occ,
        metric_root,
        (((1,), (1,)), ((), ())),
        precision=precise,
        preferred_element_type=jnp.float32,
    ).reshape(batch_count, virt_local, aux_total)
    own = lax.psum_scatter(partial_term, "aux", scatter_dimension=1, tiled=True)
    rows = lax.all_gather(own, "aux", axis=1, tiled=True)
    cols = lax.all_gather(own, "virt", axis=1, tiled=True)
    col_count = virt_count * share
    rows2 = rows.reshape(batch_count * virt_local, aux_total)
    cols2 = cols.reshape(batch_count * col_count, aux_total)
    pair = lax.dot_general(
        rows2,
        cols2,
        (((1,), (1,)), ((), ())),
        precision=precise,
        preferred_element_type=jnp.float32,
    ).reshape(batch_count, virt_local, batch_count, col_count)
    swapped = pair.transpose(2, 1, 0, 3)
    denominator = (
        occ_levels[:, None, None, None]
        + occ_levels[None, None, :, None]
        - row_levels[None, :, None, None]
        - col_levels[None, None, None, :]
    )
    weighted = ((2.0 * pair - swapped) / denominator).reshape(
        batch_count * virt_local, batch_count * col_count
    )
    density = jnp.dot(weighted, cols2, precision=precise, preferred_element_type=jnp.float32)
    result = lax.psum_scatter(density, "aux", scatter_dimension=1, tiled=True)
    return result.reshape(batch_count, virt_local, aux_local).transpose(1, 0, 2)


def solution(mesh):
    return jax.shard_map(
        shards,
        mesh=mesh,
        in_specs=(P("virt", None, "aux"), P(None, "aux"), P(), P(), P(), P()),
        out_specs=P("virt", None, "aux"),
        check_vma=False,
    )
```

time: 1110 us -> 496 us (0.45); the launches traced: 1090 us -> 496 us
  waiting for transfers between devices: 696 us -> 412 us
  local copies, waits for them, and re-layouts: 256 us -> 6.95 us
  matrix products: 110 us -> 61.9 us
  other arithmetic: 17.3 us -> 1.99 us
    psum x2 -> x0, waiting for transfers between devices: 628 us -> none  [the longest x1 480 us: from_root(): return lax.psum(block, axis)]
    all_gather x0 -> x2, waiting for transfers between devices: none -> 272 us  [the longest x1 217 us: shards(): cols = lax.all_gather(own, 'virt', axis=1, tiled=True)]
    reshape x4 -> x1, local copies, waits for them, and re-layouts: 225 us -> 0.08 us  [shards(): virt_levels.reshape(virt_count, aux_count, share)]
    reduce_scatter x1 -> x2, waiting for transfers between devices: 68.2 us -> 139 us  [the longest x1 71.8 us: shards(): own = lax.psum_scatter(partial_term, 'aux', scatter_dimension=1, tiled=True)]
    dot_general x3, matrix products: 110 us -> 61.9 us  [the longest x1 26.5 us: shards(): lax.dot_general(rows2, cols2, (((1,), (1,)), ((), ())), precision=precise...]
  transfers between devices with their start and end apart: 3 -> 4, of which waited for: 3 -> 4; matrix products, arithmetic and copies ran while one was open for 0% -> 0% of each run, Pallas kernels for 0% -> 0%
where the time goes in v1:
time: 496 us
  waiting for transfers between devices  412 us (83%)
  matrix products  61.9 us (12%)
  between operations  13.3 us (3%)
  local copies, waits for them, and re-layouts  6.95 us (1%)
    all_gather x1, waiting for transfers between devices, shards(): cols = lax.all_gather(own, 'virt', axis=1, tiled=True)  217 us
    reduce_scatter x1, waiting for transfers between devices, shards(): own = lax.psum_scatter(partial_term, 'aux', scatter_dimension=1, tiled=True)  71.8 us
    reduce_scatter x1, waiting for transfers between devices, shards(): result = lax.psum_scatter(density, 'aux', scatter_dimension=1, tiled=True)  67.3 us
    all_gather x1, waiting for transfers between devices, shards(): rows = lax.all_gather(own, 'aux', axis=1, tiled=True)  54.9 us
    dot_general x1, matrix products, shards(): lax.dot_general(rows2, cols2, (((1,), (1,)), ((), ())), precision=precise...  26.5 us
    dot_general x1, matrix products, shards(): jnp.dot(weighted, cols2, precision=precise, preferred_element_type=jnp.fl...  21.9 us
    dot_general x1, matrix products, shards(): lax.dot_general(by_occ, metric_root, (((1,), (1,)), ((), ())), precision=...  13.6 us
  transfers between devices with their start and end apart: 4, of which 4 were waited for; matrix products, arithmetic and copies ran while one was open for 0% of the time, Pallas kernels for 0%

profile of v1, /device:TPU:0, one launch (start us, length us, event | category | flops | bytes accessed | tf_op | source)
XLA Modules:
  0.0 496.3 jit_solution(10325290403499456525)
XLA Ops:
  6.5 0.0 copy-start
  6.5 1.5 copy-done
  8.1 13.6 %fusion.3 = f32[6,128,2560]{2,1,0:T(8,128)} fusion(f32[2560,640]{1,0:T(8,128)} %param.7, f32[128,6,640]{2,0,1:T(8,128)S(1)} %copy-done), kind=kOutput, calls=%fused_computation.3 | convolution fusion | flops 7549747200 | bytes 16384000 | tf_op jit(solution)/shard_map/dot_general | solution.py:32
  21.6 0.0 reduce-scatter.3.cloned.1.call-update
  21.7 0.0 all-gather.3.cloned.1.call-start
  21.7 71.8 %reduce-scatter.3.cloned.1.call-done = f32[6,32,2560]{2,1,0:T(8,128)} async-done(((f32[6,128,2560]{2,1,0:T(8,128)}), f32[6,32,2560]{2,1,0:T(8,128)}) %reduce-scatter.3.cloned.1.call-update) | async-done | bytes 1966096 | tf_op jit(solution)/shard_map/reduce_scatter | solution.py:39
  93.5 0.0 all-gather.3.cloned.1.call-update
  93.5 0.0 all-gather.5.cloned.1.call-start
  93.6 0.7 all-gather.5.cloned.1.call-update
  94.3 0.0 reduce-scatter.5.cloned.1.call-start
  94.4 0.7 select_reduce_fusion
  95.0 0.1 reshape.65
  95.1 0.1 sub.41
  95.2 0.1 dynamic_slice.6
  95.3 0.0 copy-done.4
  95.3 0.2 select_reduce_fusion.1
  95.5 0.1 broadcast_add_fusion
  95.5 0.1 broadcast_subtract_fusion
  95.6 54.9 %all-gather.3.cloned.1.call-done = f32[6,128,2560]{2,1,0:T(8,128)} async-done(((f32[6,32,2560]{2,1,0:T(8,128)}), f32[6,128,2560]{2,1,0:T(8,128)}) %all-gather.3.cloned.1.call-update) | async-done | bytes 7864336 | tf_op jit(solution)/shard_map/all_gather | solution.py:40
  150.5 217.3 %all-gather.5.cloned.1.call-done = f32[6,256,2560]{2,1,0:T(8,128)} async-done(((f32[6,32,2560]{2,1,0:T(8,128)}), f32[6,256,2560]{2,1,0:T(8,128)}) %all-gather.5.cloned.1.call-update) | async-done | bytes 15728656 | tf_op jit(solution)/shard_map/all_gather | solution.py:41
  367.8 26.5 %fusion = f32[6,128,6,256]{3,1,2,0:T(8,128)S(1)} fusion(f32[6,256,2560]{2,1,0:T(8,128)} %all-gather.5.cloned.1.call-done, f32[6,128,2560]{2,1,0:T(8,128)} %all-gather.3.cloned.1.call-done), kind=kOutput, calls=%fused_computation | convolution fusion | flops 18119393280 | bytes 28311552 | tf_op jit(solution)/shard_map/dot_general | solution.py:45
  394.3 0.0 slice-start
  394.3 0.0 slice-start.1
  394.3 1.0 fusion.5
  395.3 0.0 slice-start.2
  395.3 2.8 copy.11
  398.1 0.0 slice-start.3
  398.1 2.3 copy.13
  400.5 0.0 copy-start.1
  400.5 21.9 %fusion.7 = f32[768,2560]{1,0:T(8,128)} fusion(f32[768,1536]{1,0:T(8,128)S(1)} %bitcast.28, f32[1536,2560]{1,0:T(8,128)S(1)} %bitcast.31), kind=kOutput, calls=%fused_computation.16 | convolution fusion | flops 18119393280 | bytes 28311552 | tf_op jit(solution)/shard_map/dot_general | solution.py:62
  422.4 0.0 reduce-scatter.5.cloned.1.call-update
  422.4 67.3 %reduce-scatter.5.cloned.1.call-done = f32[768,640]{1,0:T(8,128)} async-done(((f32[768,2560]{1,0:T(8,128)}), f32[768,640]{1,0:T(8,128)}) %reduce-scatter.5.cloned.1.call-update) | async-done | bytes 1966096 | tf_op jit(solution)/shard_map/reduce_scatter | solution.py:63
  (15 shorter events, 0.1 us)
Async XLA Ops:
  6.5 1.5 copy-start
  6.5 87.0 %reduce-scatter.3.cloned.1.call-start = ((), (), s32[]{:S(2)}) async-start(), calls=%async_computation.2 | async-start | bytes 9830400 | tf_op jit(solution)/shard_map/reduce_scatter | solution.py:39
  21.6 72.7 %copy-start.2 = (f32[1024]{0:T(1024)S(1)}, f32[1024]{0:T(1024)}, u32[]{:S(2)}) copy-start(f32[1024]{0:T(1024)} %param.9) | copy-start | bytes 12292
  21.6 72.7 %copy-start.3 = (s32[1024]{0:T(1024)S(1)}, s32[1024]{0:T(1024)}, u32[]{:S(2)}) copy-start(s32[1024]{0:T(1024)} %param.11) | copy-start | bytes 12292
  21.6 73.6 %copy-start.4 = (f32[256]{0:T(256)S(1)}, f32[256]{0:T(256)}, u32[]{:S(2)}) copy-start(f32[256]{0:T(256)} %param.8) | copy-start | bytes 3076
  21.6 73.6 %copy-start.5 = (s32[6]{0:T(128)S(1)}, s32[6]{0:T(128)}, u32[]{:S(2)}) copy-start(s32[6]{0:T(128)} %param.10) | copy-start | bytes 76
  21.7 128.8 %all-gather.3.cloned.1.call-start = ((), (), s32[]{:S(2)}) async-start(), calls=%async_computation.3 | async-start | bytes 9830400 | tf_op jit(solution)/shard_map/all_gather | solution.py:40
  93.5 274.2 %all-gather.5.cloned.1.call-start = ((), (), s32[]{:S(2)}) async-start(), calls=%async_computation.4 | async-start | bytes 17694720 | tf_op jit(solution)/shard_map/all_gather | solution.py:41
  94.3 395.5 %reduce-scatter.5.cloned.1.call-start = ((), (), s32[]{:S(2)}) async-start(), calls=%async_computation.5 | async-start | bytes 9830400 | tf_op jit(solution)/shard_map/reduce_scatter | solution.py:63
  394.3 6.2 %slice-start = ((s8[15728640]{0:T(1024)(128)(4,1)}), s8[4194304]{0:T(1024)(128)(4,1)S(1)}, s32[]{:S(2)}) async-start(s8[15728640]{0:T(1024)(128)(4,1)} %bitcast.29), calls=%async_computation.6 | async-start | bytes 8388608
  394.3 6.2 %slice-start.1 = ((s8[15728640]{0:T(1024)(128)(4,1)}), s8[3145728]{0:T(1024)(128)(4,1)S(1)}, s32[]{:S(2)}) async-start(s8[15728640]{0:T(1024)(128)(4,1)} %bitcast.29), calls=%async_computation.7 | async-start | bytes 6291456
  395.3 5.2 %slice-start.2 = ((s8[15728640]{0:T(1024)(128)(4,1)}), s8[4194304]{0:T(1024)(128)(4,1)S(1)}, s32[]{:S(2)}) async-start(s8[15728640]{0:T(1024)(128)(4,1)} %bitcast.29), calls=%async_computation.8 | async-start | bytes 8388608
  398.1 2.4 slice-start.3
  400.5 89.2 %copy-start.1 = (f32[128,6,640]{2,0,1:T(8,128)S(1)}, f32[128,6,640]{2,0,1:T(8,128)}, u32[]{:S(2)}) copy-start(f32[128,6,640]{2,0,1:T(8,128)} %param.6) | copy-start | bytes 5898244
Sparse Core Ops, SparseCore 0:
  21.8 71.6 reduce-scatter.2
  95.2 55.2 all-gather.2
  152.9 214.7 all-gather.4
  422.5 67.1 reduce-scatter.4

commit v2 on v1

--- a/solution.py
+++ b/solution.py
@@ -1,6 +1,10 @@
+import functools
+
 import jax
 import jax.numpy as jnp
 from jax import lax
+from jax.experimental import pallas as pl
+from jax.experimental.pallas import tpu as pltpu
 from jax.sharding import PartitionSpec as P
 
 precise = lax.Precision.HIGH
@@ -11,6 +15,171 @@
     return jnp.sum(
         jnp.where(picked[:, None] == places[None, :], levels_table[None, :], 0.0), axis=1
     )
+
+
+def ring_member(place, count):
+    return jnp.where(place < count // 2, 2 * place, 2 * (count - 1 - place) + 1)
+
+
+def ring_place(member, count):
+    return jnp.where(lax.rem(member, 2) == 0, member // 2, count - 1 - member // 2)
+
+
+def gather_kernel(
+    aux_count, virt_count, partial, rows, cols, pairsum, arrived, own,
+    sib_send, sib_recv, far_send, far_recv, row_send, row_recv, pass_send, pass_recv,
+    ring_send, ring_recv, local_sem,
+):
+    occs, far_count, _, share, _ = partial.shape
+    aux_place = lax.axis_index("aux")
+    virt_place = lax.axis_index("virt")
+    core = lax.rem(aux_place, 2)
+    far_place = aux_place // 2
+    sibling = {"aux": far_place * 2 + 1 - core}
+    fars = [lax.rem(far_place + hop, far_count) for hop in range(1, far_count)]
+    place = ring_place(virt_place, virt_count)
+    ahead = {"virt": ring_member(lax.rem(place + 1, virt_count), virt_count)}
+    behind = {"virt": ring_member(lax.rem(place + virt_count - 1, virt_count), virt_count)}
+
+    def remote(source, target, send, recv, device):
+        return pltpu.make_async_remote_copy(
+            src_ref=source, dst_ref=target, send_sem=send, recv_sem=recv,
+            device_id=device, device_id_type=pl.DeviceIdType.MESH,
+        )
+
+    barrier = pltpu.get_barrier_semaphore()
+    partners = [sibling, ahead, behind] + [{"aux": far * 2 + core} for far in fars]
+    for partner in partners:
+        pl.semaphore_signal(barrier, inc=1, device_id=partner, device_id_type=pl.DeviceIdType.MESH)
+    pl.semaphore_wait(barrier, len(partners))
+
+    forward = (occs + 1) // 2
+    order = []
+    for occ in range(forward):
+        order.append(occ)
+        if forward + occ < occs:
+            order.append(forward + occ)
+
+    sib_copies = {}
+    for occ in order:
+        copy = remote(
+            partial.at[occ, :, 1 - core], pairsum.at[occ], sib_send.at[occ], sib_recv.at[occ], sibling
+        )
+        copy.start()
+        sib_copies[occ] = copy
+    far_copies = {}
+    for occ in order:
+        sib_copies[occ].wait_recv()
+        pairsum[occ] = pairsum[occ] + partial[occ, :, core]
+        for hop, far in enumerate(fars):
+            copy = remote(
+                pairsum.at[occ, far], arrived.at[occ, hop], far_send.at[occ, hop],
+                far_recv.at[occ, hop], {"aux": far * 2 + core},
+            )
+            copy.start()
+            far_copies[occ, hop] = copy
+
+    def ring_copy(occ, step):
+        cw = occ < forward
+        origin = lax.rem(place + (virt_count - step if cw else step), virt_count)
+        slot = cols.at[occ, pl.ds(pl.multiple_of(ring_member(origin, virt_count) * share, share), share)]
+        source = own.at[occ] if step == 0 else slot
+        return remote(
+            source, slot, ring_send.at[occ, step], ring_recv.at[occ, step], ahead if cw else behind
+        )
+
+    def row_slot(occ, member):
+        return rows.at[occ, pl.ds(pl.multiple_of(member * share, share), share)]
+
+    ring = {}
+    row_copies = {}
+    pass_copies = {}
+    local = []
+    for occ in order:
+        for hop in range(len(fars)):
+            far_copies[occ, hop].wait_recv()
+        total = pairsum[occ, far_place]
+        for hop in range(len(fars)):
+            total = total + arrived[occ, hop]
+        own[occ] = total
+        ring[occ, 0] = ring_copy(occ, 0)
+        ring[occ, 0].start()
+        for hop, far in enumerate(fars):
+            copy = remote(
+                own.at[occ], row_slot(occ, aux_place), row_send.at[occ, hop],
+                row_recv.at[occ, hop], {"aux": far * 2 + core},
+            )
+            copy.start()
+            row_copies[occ, hop] = copy
+        copy = remote(
+            own.at[occ], row_slot(occ, aux_place), pass_send.at[occ, 0], pass_recv.at[occ, 0], sibling
+        )
+        copy.start()
+        pass_copies[occ, 0] = copy
+        copy = pltpu.make_async_copy(own.at[occ], row_slot(occ, aux_place), local_sem.at[occ, 0])
+        copy.start()
+        local.append(copy)
+        mine = cols.at[occ, pl.ds(pl.multiple_of(virt_place * share, share), share)]
+        copy = pltpu.make_async_copy(own.at[occ], mine, local_sem.at[occ, 1])
+        copy.start()
+        local.append(copy)
+
+    for step in range(1, virt_count - 1):
+        for occ in order:
+            ring[occ, step - 1].wait_recv()
+            ring[occ, step] = ring_copy(occ, step)
+            ring[occ, step].start()
+        if step == 3:
+            for occ in order:
+                for hop in range(len(fars)):
+                    row_copies[occ, hop].wait_recv()
+                    sender = lax.rem(far_place + far_count - 1 - hop, far_count) * 2 + core
+                    copy = remote(
+                        row_slot(occ, sender), row_slot(occ, sender), pass_send.at[occ, hop + 1],
+                        pass_recv.at[occ, hop + 1], sibling,
+                    )
+                    copy.start()
+                    pass_copies[occ, hop + 1] = copy
+    for occ in order:
+        ring[occ, virt_count - 2].wait_recv()
+    for copy in pass_copies.values():
+        copy.wait_recv()
+    for copy in local:
+        copy.wait()
+    for group in (sib_copies, far_copies, ring, row_copies, pass_copies):
+        for copy in group.values():
+            copy.wait_send()
+
+
+def gather_fitted(partial_term, aux_count, virt_count):
+    occs, virt_local, aux_total = partial_term.shape
+    share = virt_local // aux_count
+    far_count = aux_count // 2
+    dma = pltpu.SemaphoreType.DMA
+    return pl.pallas_call(
+        functools.partial(gather_kernel, aux_count, virt_count),
+        out_shape=(
+            jax.ShapeDtypeStruct((occs, virt_local, aux_total), jnp.float32),
+            jax.ShapeDtypeStruct((occs, virt_count * share, aux_total), jnp.float32),
+        ),
+        in_specs=[pl.BlockSpec(memory_space=pltpu.VMEM)],
+        out_specs=(pl.BlockSpec(memory_space=pl.ANY), pl.BlockSpec(memory_space=pl.ANY)),
+        scratch_shapes=[
+            pltpu.VMEM((occs, far_count, share, aux_total), jnp.float32),
+            pltpu.VMEM((occs, far_count - 1, share, aux_total), jnp.float32),
+            pltpu.VMEM((occs, share, aux_total), jnp.float32),
+            dma((occs,)), dma((occs,)),
+            dma((occs, far_count - 1)), dma((occs, far_count - 1)),
+            dma((occs, far_count - 1)), dma((occs, far_count - 1)),
+            dma((occs, far_count)), dma((occs, far_count)),
+            dma((occs, virt_count - 1)), dma((occs, virt_count - 1)),
+            dma((occs, 2)),
+        ],
+        compiler_params=pltpu.CompilerParams(
+            collective_id=0, has_side_effects=True, vmem_limit_bytes=40 * 1024 * 1024
+        ),
+        cost_estimate=pl.CostEstimate(flops=0, bytes_accessed=4 * 6 * occs * virt_local * aux_total, transcendentals=0),
+    )(partial_term.reshape(occs, far_count, 2, share, aux_total))
 
 
 def shards(integrals, metric_root, occ_energy, virt_energy, batch_index, virt_order):
@@ -36,9 +205,7 @@
         precision=precise,
         preferred_element_type=jnp.float32,
     ).reshape(batch_count, virt_local, aux_total)
-    own = lax.psum_scatter(partial_term, "aux", scatter_dimension=1, tiled=True)
-    rows = lax.all_gather(own, "aux", axis=1, tiled=True)
-    cols = lax.all_gather(own, "virt", axis=1, tiled=True)
+    rows, cols = gather_fitted(partial_term, aux_count, virt_count)
     col_count = virt_count * share
     rows2 = rows.reshape(batch_count * virt_local, aux_total)
     cols2 = cols.reshape(batch_count * col_count, aux_total)

time: 496 us -> 347 us (0.70)
  waiting for transfers between devices: 412 us -> 68.3 us
  Pallas kernels: 0 us -> 191 us
    all_gather x2 -> x0, waiting for transfers between devices: 272 us -> none  [the longest x1 217 us: shards(): cols = lax.all_gather(own, 'virt', axis=1, tiled=True)]
    pallas_call x0 -> x1, Pallas kernels: none -> 191 us  [gather_fitted(): pl.pallas_call(functools.partial(gather_kernel, aux_count, virt_count), o...]
    reduce_scatter x1 -> x0, waiting for transfers between devices: 71.8 us -> none  [shards(): own = lax.psum_scatter(partial_term, 'aux', scatter_dimension=1, tiled=True)]
  transfers between devices with their start and end apart: 4 -> 1, of which waited for: 4 -> 1; matrix products, arithmetic and copies ran while one was open for 0% -> 0% of each run, Pallas kernels for 0% -> 0%
where the time goes in v2:
time: 347 us; the launch traced here: 346 us
  Pallas kernels  191 us (55%)
  waiting for transfers between devices  68.3 us (20%)
  matrix products  62 us (18%)
  between operations  13.5 us (4%)
  local copies, waits for them, and re-layouts  10 us (3%)
    pallas_call x1, Pallas kernels, gather_fitted(): pl.pallas_call(functools.partial(gather_kernel, aux_count, virt_count), o...  191 us
    reduce_scatter x1, waiting for transfers between devices, shards(): result = lax.psum_scatter(density, 'aux', scatter_dimension=1, tiled=True)  68.3 us
    dot_general x1, matrix products, shards(): lax.dot_general(rows2, cols2, (((1,), (1,)), ((), ())), precision=precise...  26.6 us
    dot_general x1, matrix products, shards(): jnp.dot(weighted, cols2, precision=precise, preferred_element_type=jnp.fl...  21.9 us
    dot_general x1, matrix products, shards(): lax.dot_general(by_occ, metric_root, (((1,), (1,)), ((), ())), precision=...  13.5 us
    unnamed x23, local copies, waits for them, and re-layouts  7.02 us
  transfers between devices with their start and end apart: 1, of which 1 were waited for; matrix products, arithmetic and copies ran while one was open for 0% of the time, Pallas kernels for 0%

profile of v2, /device:TPU:0, one launch (start us, length us, event | category | flops | bytes accessed | tf_op | source)
XLA Modules:
  0.0 346.4 jit_solution(14906201427069592273)
XLA Ops:
  6.5 0.0 copy-start
  6.5 0.0 reduce-scatter.2.cloned.1.call-start
  6.5 1.5 copy-done
  8.1 13.5 %fusion.3.partial = f32[6,2,2,32,2560]{4,3,2,1,0:T(8,128)} fusion(f32[6,2,2,32,640]{4,3,2,1,0:T(8,128)S(1)} %bitcast.30, f32[2560,640]{1,0:T(8,128)} %param.7), kind=kOutput, calls=%fused_computation.3 | convolution fusion | flops 7549747200 | bytes 16384000 | tf_op jit(solution)/shard_map/dot_general | solution.py:201
  21.6 190.6 %shard_map.64 = (f32[6,128,2560]{2,1,0:T(8,128)S(1)}, f32[6,256,2560]{2,1,0:T(8,128)}) custom-call(f32[6,2,2,32,2560]{4,3,2,1,0:T(8,128)} %fusion.3.partial), custom_call_target="tpu_custom_call" | custom-call | bytes 47185920 | tf_op jit(solution)/shard_map/pallas_call | solution.py:159
  212.2 0.0 copy-start.2
  212.2 3.1 copy-done.2
  215.3 0.0 copy-done.3
  215.3 0.0 copy-done.4
  215.3 0.7 select_reduce_fusion
  216.0 0.1 reshape.64
  216.1 0.1 sub.41
  216.2 0.1 dynamic_slice.6
  216.2 0.0 copy-done.5
  216.2 0.0 copy-done.6
  216.2 0.2 select_reduce_fusion.1
  216.4 0.1 broadcast_add_fusion
  216.5 26.6 %fusion = f32[6,128,6,256]{3,1,2,0:T(8,128)S(1)} fusion(f32[6,256,2560]{2,1,0:T(8,128)} %get-tuple-element.8, f32[6,128,2560]{2,1,0:T(8,128)} %copy-done.2), kind=kOutput, calls=%fused_computation | convolution fusion | flops 18119393280 | bytes 28311552 | tf_op jit(solution)/shard_map/dot_general | solution.py:212
  243.1 0.1 broadcast_subtract_fusion
  243.2 1.0 fusion.5
  244.2 0.0 slice-start.2
  244.2 2.8 copy.11
  247.0 0.0 slice-start.3
  247.0 2.3 copy.14
  249.3 0.0 slice-done
  249.4 0.0 slice-done.1
  249.4 0.0 slice-done.2
  249.4 0.0 slice-done.3
  249.4 0.0 copy-start.1
  249.4 21.9 %fusion.6 = f32[768,2560]{1,0:T(8,128)} fusion(f32[768,1536]{1,0:T(8,128)S(1)} %bitcast.32, f32[1536,2560]{1,0:T(8,128)S(1)} %bitcast.35), kind=kOutput, calls=%fused_computation.15 | convolution fusion | flops 18119393280 | bytes 28311552 | tf_op jit(solution)/shard_map/dot_general | solution.py:229
  271.3 0.0 reduce-scatter.2.cloned.1.call-update
  271.3 68.3 %reduce-scatter.2.cloned.1.call-done = f32[768,640]{1,0:T(8,128)} async-done(((f32[768,2560]{1,0:T(8,128)}), f32[768,640]{1,0:T(8,128)}) %reduce-scatter.2.cloned.1.call-update) | async-done | bytes 1966096 | tf_op jit(solution)/shard_map/reduce_scatter | solution.py:230
  (9 shorter events, 0.0 us)
Async XLA Ops:
  6.5 1.5 copy-start
  6.5 333.1 %reduce-scatter.2.cloned.1.call-start = ((), (), s32[]{:S(2)}) async-start(), calls=%async_computation.1 | async-start | bytes 9830400 | tf_op jit(solution)/shard_map/reduce_scatter | solution.py:230
  21.6 193.7 %copy-start.3 = (f32[1024]{0:T(1024)S(1)}, f32[1024]{0:T(1024)}, u32[]{:S(2)}) copy-start(f32[1024]{0:T(1024)} %param.9) | copy-start | bytes 12292
  21.6 193.7 %copy-start.4 = (s32[1024]{0:T(1024)S(1)}, s32[1024]{0:T(1024)}, u32[]{:S(2)}) copy-start(s32[1024]{0:T(1024)} %param.11) | copy-start | bytes 12292
  21.6 194.6 %copy-start.5 = (f32[256]{0:T(256)S(1)}, f32[256]{0:T(256)}, u32[]{:S(2)}) copy-start(f32[256]{0:T(256)} %param.8) | copy-start | bytes 3076
  21.6 194.6 %copy-start.6 = (s32[6]{0:T(128)S(1)}, s32[6]{0:T(128)}, u32[]{:S(2)}) copy-start(s32[6]{0:T(128)} %param.10) | copy-start | bytes 76
  212.2 3.1 copy-start.2
  243.2 6.2 %slice-start = ((s8[15728640]{0:T(1024)(128)(4,1)}), s8[4194304]{0:T(1024)(128)(4,1)S(1)}, s32[]{:S(2)}) async-start(s8[15728640]{0:T(1024)(128)(4,1)} %bitcast.33), calls=%async_computation.2 | async-start | bytes 8388608
  243.2 6.2 %slice-start.1 = ((s8[15728640]{0:T(1024)(128)(4,1)}), s8[3145728]{0:T(1024)(128)(4,1)S(1)}, s32[]{:S(2)}) async-start(s8[15728640]{0:T(1024)(128)(4,1)} %bitcast.33), calls=%async_computation.3 | async-start | bytes 6291456
  244.2 5.2 %slice-start.2 = ((s8[15728640]{0:T(1024)(128)(4,1)}), s8[4194304]{0:T(1024)(128)(4,1)S(1)}, s32[]{:S(2)}) async-start(s8[15728640]{0:T(1024)(128)(4,1)} %bitcast.33), calls=%async_computation.4 | async-start | bytes 8388608
  247.0 2.4 slice-start.3
  249.4 90.2 %copy-start.1 = (f32[128,6,640]{2,0,1:T(8,128)S(1)}, f32[128,6,640]{2,0,1:T(8,128)}, u32[]{:S(2)}) copy-start(f32[128,6,640]{2,0,1:T(8,128)} %param.6) | copy-start | bytes 5898244
Sparse Core Ops, SparseCore 0:
  271.4 68.1 reduce-scatter.1

commit v3 on v2

--- a/solution.py
+++ b/solution.py
@@ -182,6 +182,157 @@
     )(partial_term.reshape(occs, far_count, 2, share, aux_total))
 
 
+def split_parts(values):
+    high = values.astype(jnp.bfloat16)
+    return high, (values - high.astype(jnp.float32)).astype(jnp.bfloat16)
+
+
+def density_kernel(
+    aux_count, pair, occ_levels, row_levels, col_levels, cols, out,
+    w_high, w_low, stage, c_high, c_low, partial, from_sib, from_far,
+    stage_sem, sib_send, sib_recv, far_send, far_recv,
+):
+    occs, virt_local, width = out.shape
+    rows = occs * virt_local
+    half = rows // 2
+    half_occs = occs // 2
+    col_count = col_levels.shape[1]
+    far_count = aux_count // 2
+    aux_place = lax.axis_index("aux")
+    core = lax.rem(aux_place, 2)
+    far_place = aux_place // 2
+    sibling = {"aux": far_place * 2 + 1 - core}
+
+    def fetch(unit, slot):
+        target = lax.rem(far_place + 1 + unit // 2, far_count)
+        owner = target * 2 + jnp.where(lax.rem(unit, 2) == 0, 1 - core, core)
+        return pltpu.make_async_copy(
+            cols.at[:, pl.ds(pl.multiple_of(owner * width, 128), width)],
+            stage.at[slot], stage_sem.at[slot],
+        )
+
+    def sib_copy(hop, part):
+        return pltpu.make_async_remote_copy(
+            src_ref=partial.at[2 * hop, part], dst_ref=from_sib.at[hop, part],
+            send_sem=sib_send.at[hop, part], recv_sem=sib_recv.at[hop, part],
+            device_id=sibling, device_id_type=pl.DeviceIdType.MESH,
+        )
+
+    def far_copy(hop, part):
+        target = lax.rem(far_place + 1 + hop, far_count)
+        return pltpu.make_async_remote_copy(
+            src_ref=partial.at[2 * hop + 1, part], dst_ref=from_far.at[hop, part],
+            send_sem=far_send.at[hop, part], recv_sem=far_recv.at[hop, part],
+            device_id={"aux": target * 2 + core}, device_id_type=pl.DeviceIdType.MESH,
+        )
+
+    barrier = pltpu.get_barrier_semaphore()
+    partners = [sibling] + [
+        {"aux": lax.rem(far_place + hop, far_count) * 2 + core} for hop in range(1, far_count)
+    ]
+    for partner in partners:
+        pl.semaphore_signal(barrier, inc=1, device_id=partner, device_id_type=pl.DeviceIdType.MESH)
+    fetch(0, 0).start()
+
+    for i in range(occs):
+        for j in range(occs):
+            direct = pair[pl.ds(i * virt_local, virt_local), pl.ds(j * col_count, col_count)]
+            crossed = pair[pl.ds(j * virt_local, virt_local), pl.ds(i * col_count, col_count)]
+            denominator = occ_levels[i] + occ_levels[j] - row_levels[...] - col_levels[...]
+            high, low = split_parts((2.0 * direct - crossed) / denominator)
+            w_high[pl.ds(i * virt_local, virt_local), pl.ds(j * col_count, col_count)] = high
+            w_low[pl.ds(i * virt_local, virt_local), pl.ds(j * col_count, col_count)] = low
+    pl.semaphore_wait(barrier, len(partners))
+
+    depth = w_high.shape[1]
+    units = 2 * far_count
+    pieces = occs
+    piece = depth // pieces
+    for unit in range(units):
+        slot = unit % 2
+        hop = unit // 2
+        if unit + 1 < units:
+            fetch(unit + 1, 1 - slot).start()
+        fetch(unit, slot).wait()
+
+        @pl.loop(0, pieces)
+        def _(step):
+            where = pl.ds(pl.multiple_of(step * piece, piece), piece)
+            high, low = split_parts(stage[slot, where, :])
+            c_high[where, :] = high
+            c_low[where, :] = low
+
+        @pl.loop(0, 2)
+        def _(part):
+            where = pl.ds(pl.multiple_of(part * half, half), half)
+            left_high = w_high[where, :]
+            right_high = c_high[...]
+            total = jnp.dot(left_high, c_low[...], preferred_element_type=jnp.float32)
+            total += jnp.dot(w_low[where, :], right_high, preferred_element_type=jnp.float32)
+            total += jnp.dot(left_high, right_high, preferred_element_type=jnp.float32)
+            if unit % 2 == 0:
+                partial[unit, part] = total
+                sib_copy(hop, part).start()
+            elif hop < far_count - 1:
+                sib_copy(hop, part).wait_recv()
+                partial[unit, part] = total + from_sib[hop, part]
+                far_copy(hop, part).start()
+            else:
+                sib_copy(hop, part).wait_recv()
+                partial[unit, part] = total + from_sib[hop, part]
+
+    for part in range(2):
+        total = partial[units - 1, part]
+        for hop in range(far_count - 1):
+            far_copy(hop, part).wait_recv()
+            total = total + from_far[hop, part]
+        out[pl.ds(part * half_occs, half_occs)] = total.reshape(half_occs, virt_local, width)
+    for part in range(2):
+        for hop in range(far_count):
+            sib_copy(hop, part).wait_send()
+        for hop in range(far_count - 1):
+            far_copy(hop, part).wait_send()
+
+
+def scattered_density(pair, occ_levels, row_levels, col_levels, cols, aux_count):
+    occs = occ_levels.shape[0]
+    virt_local = row_levels.shape[0]
+    rows, depth = pair.shape
+    width = cols.shape[1] // aux_count
+    far_count = aux_count // 2
+    dma = pltpu.SemaphoreType.DMA
+    vmem = pl.BlockSpec(memory_space=pltpu.VMEM)
+    return pl.pallas_call(
+        functools.partial(density_kernel, aux_count),
+        out_shape=jax.ShapeDtypeStruct((occs, virt_local, width), jnp.float32),
+        in_specs=[
+            vmem, pl.BlockSpec(memory_space=pltpu.SMEM), vmem, vmem,
+            pl.BlockSpec(memory_space=pl.ANY),
+        ],
+        out_specs=vmem,
+        scratch_shapes=[
+            pltpu.VMEM((rows, depth), jnp.bfloat16),
+            pltpu.VMEM((rows, depth), jnp.bfloat16),
+            pltpu.VMEM((2, depth, width), jnp.float32),
+            pltpu.VMEM((depth, width), jnp.bfloat16),
+            pltpu.VMEM((depth, width), jnp.bfloat16),
+            pltpu.VMEM((2 * far_count, 2, rows // 2, width), jnp.float32),
+            pltpu.VMEM((far_count, 2, rows // 2, width), jnp.float32),
+            pltpu.VMEM((far_count - 1, 2, rows // 2, width), jnp.float32),
+            dma((2,)),
+            dma((far_count, 2)), dma((far_count, 2)),
+            dma((far_count - 1, 2)), dma((far_count - 1, 2)),
+        ],
+        compiler_params=pltpu.CompilerParams(
+            collective_id=1, has_side_effects=True, vmem_limit_bytes=50 * 1024 * 1024
+        ),
+        cost_estimate=pl.CostEstimate(
+            flops=6 * rows * depth * cols.shape[1], bytes_accessed=4 * depth * cols.shape[1],
+            transcendentals=0,
+        ),
+    )(pair, occ_levels, row_levels[:, None], col_levels[None, :], cols)
+
+
 def shards(integrals, metric_root, occ_energy, virt_energy, batch_index, virt_order):
     virt_local, batch_count, aux_local = integrals.shape
     aux_total = metric_root.shape[0]
@@ -215,7 +366,11 @@
         (((1,), (1,)), ((), ())),
         precision=precise,
         preferred_element_type=jnp.float32,
-    ).reshape(batch_count, virt_local, batch_count, col_count)
+    )
+    if aux_local % 128 == 0 and batch_count % 2 == 0:
+        result = scattered_density(pair, occ_levels, row_levels, col_levels, cols2, aux_count)
+        return result.transpose(1, 0, 2)
+    pair = pair.reshape(batch_count, virt_local, batch_count, col_count)
     swapped = pair.transpose(2, 1, 0, 3)
     denominator = (
         occ_levels[:, None, None, None]

time: 347 us -> 291 us (0.84)
  waiting for transfers between devices: 68.3 us -> 0 us
  Pallas kernels: 191 us -> 251 us
  matrix products: 62 us -> 36.4 us
  between operations: 13.5 us -> 0.08 us
  local copies, waits for them, and re-layouts: 10 us -> 3.21 us
    reduce_scatter x1 -> x0, waiting for transfers between devices: 68.3 us -> none  [shards(): result = lax.psum_scatter(density, 'aux', scatter_dimension=1, tiled=True)]
    pallas_call x0 -> x1, Pallas kernels: none -> 60.1 us  [scattered_density(): pl.pallas_call(functools.partial(density_kernel, aux_count), out_shape=ja...]
    dot_general x1 -> x0, matrix products: 21.9 us -> none  [shards(): jnp.dot(weighted, cols2, precision=precise, preferred_element_type=jnp.fl...]
    unnamed x23 -> x11, local copies, waits for them, and re-layouts: 7.02 us -> 2.84 us
    dot_general x1, matrix products: 26.6 us -> 22.8 us  [shards(): lax.dot_general(rows2, cols2, (((1,), (1,)), ((), ())), precision=precise...]
  transfers between devices with their start and end apart: 1 -> 0, of which waited for: 1 -> 0; matrix products, arithmetic and copies ran while one was open for 0% -> 0% of each run, Pallas kernels for 0% -> 0%
where the time goes in v3:
time: 291 us
  Pallas kernels  251 us (86%)
  matrix products  36.4 us (13%)
  local copies, waits for them, and re-layouts  3.21 us (1%)
    pallas_call x1, Pallas kernels, gather_fitted(): pl.pallas_call(functools.partial(gather_kernel, aux_count, virt_count), o...  191 us
    pallas_call x1, Pallas kernels, scattered_density(): pl.pallas_call(functools.partial(density_kernel, aux_count), out_shape=ja...  60.1 us
    dot_general x1, matrix products, shards(): lax.dot_general(rows2, cols2, (((1,), (1,)), ((), ())), precision=precise...  22.8 us
    dot_general x1, matrix products, shards(): lax.dot_general(by_occ, metric_root, (((1,), (1,)), ((), ())), precision=...  13.6 us

profile of v3, /device:TPU:0, one launch (start us, length us, event | category | flops | bytes accessed | tf_op | source)
XLA Modules:
  0.0 291.2 jit_solution(1260506321426348974)
XLA Ops:
  0.0 0.0 copy-start
  0.0 1.5 copy-done
  1.5 13.6 %fusion.partial = f32[6,2,2,32,2560]{4,3,2,1,0:T(8,128)} fusion(f32[6,2,2,32,640]{4,3,2,1,0:T(8,128)S(1)} %bitcast.16, f32[2560,640]{1,0:T(8,128)} %param.7), kind=kOutput, calls=%fused_computation | convolution fusion | flops 7549747200 | bytes 16384000 | tf_op jit(solution)/shard_map/dot_general | solution.py:352
  15.1 190.5 %shard_map.64 = (f32[6,128,2560]{2,1,0:T(8,128)S(1)}, f32[6,256,2560]{2,1,0:T(8,128)}) custom-call(f32[6,2,2,32,2560]{4,3,2,1,0:T(8,128)} %fusion.partial), custom_call_target="tpu_custom_call" | custom-call | bytes 47185920 | tf_op jit(solution)/shard_map/pallas_call | solution.py:159
  205.7 0.0 copy-start.3
  205.7 0.0 copy-start.4
  205.7 0.0 copy-start.1
  205.7 0.0 copy-start.2
  205.7 22.8 %fusion.2.pair = f32[768,1536]{1,0:T(8,128)} fusion(f32[768,2560]{1,0:T(8,128)S(1)} %bitcast.18, f32[1536,2560]{1,0:T(8,128)} %bitcast.19), kind=kOutput, calls=%fused_computation.8 | convolution fusion | flops 18119393280 | bytes 28311552 | tf_op jit(solution)/shard_map/dot_general | solution.py:363
  228.6 0.0 copy-done.3
  228.6 0.0 copy-done.4
  228.6 0.2 select_reduce_fusion.1.occ_levels
  228.8 0.0 copy-done.1
  228.8 0.0 copy-done.2
  228.8 0.7 select_reduce_fusion
  229.4 0.1 dynamic-slice_bitcast_fusion
  229.5 0.1 copy.9.row_levels
  229.6 0.1 reshape.18
  229.7 0.1 broadcast_in_dim_reshape.3.col_levels
  229.8 60.1 %shard_map.65 = f32[6,128,640]{2,1,0:T(8,128)S(1)} custom-call(f32[768,1536]{1,0:T(8,128)} %fusion.2.pair, f32[6]{0:T(128)S(1)} %select_reduce_fusion.1.occ_levels, f32[128,1]{1,0:T(8,128)S(1)} %copy.9.row_levels, f32[1,256]{1,0:T(1,128)S(1)} %broadcast_in_dim_reshape.3.col_levels, f32[1536,2560]{1,0:T(8,128)} %bitcast.20), custom_call_target="tpu_custom_call" | custom-call | flops 18119393280 | bytes 15728640 | tf_op jit(solution)/shard_map/pallas_call | solution.py:305
  289.9 1.3 copy.12
  (1 shorter events, 0.0 us)
Async XLA Ops:
  0.0 1.5 copy-start
  205.7 22.9 %copy-start.3 = (f32[256]{0:T(256)S(1)}, f32[256]{0:T(256)}, u32[]{:S(2)}) copy-start(f32[256]{0:T(256)} %param.8) | copy-start | bytes 3076
  205.7 22.9 %copy-start.4 = (s32[6]{0:T(128)S(1)}, s32[6]{0:T(128)}, u32[]{:S(2)}) copy-start(s32[6]{0:T(128)} %param.10) | copy-start | bytes 76
  205.7 23.1 %copy-start.1 = (f32[1024]{0:T(1024)S(1)}, f32[1024]{0:T(1024)}, u32[]{:S(2)}) copy-start(f32[1024]{0:T(1024)} %param.9) | copy-start | bytes 12292
  205.7 23.1 %copy-start.2 = (s32[1024]{0:T(1024)S(1)}, s32[1024]{0:T(1024)}, u32[]{:S(2)}) copy-start(s32[1024]{0:T(1024)} %param.11) | copy-start | bytes 12292

commit v4 on v3

--- a/solution.py
+++ b/solution.py
@@ -95,7 +95,7 @@
     row_copies = {}
     pass_copies = {}
     local = []
-    for occ in order:
+    def finish_sum(occ):
         for hop in range(len(fars)):
             far_copies[occ, hop].wait_recv()
         total = pairsum[occ, far_place]
@@ -104,13 +104,6 @@
         own[occ] = total
         ring[occ, 0] = ring_copy(occ, 0)
         ring[occ, 0].start()
-        for hop, far in enumerate(fars):
-            copy = remote(
-                own.at[occ], row_slot(occ, aux_place), row_send.at[occ, hop],
-                row_recv.at[occ, hop], {"aux": far * 2 + core},
-            )
-            copy.start()
-            row_copies[occ, hop] = copy
         copy = remote(
             own.at[occ], row_slot(occ, aux_place), pass_send.at[occ, 0], pass_recv.at[occ, 0], sibling
         )
@@ -124,22 +117,44 @@
         copy.start()
         local.append(copy)
 
-    for step in range(1, virt_count - 1):
-        for occ in order:
-            ring[occ, step - 1].wait_recv()
-            ring[occ, step] = ring_copy(occ, step)
-            ring[occ, step].start()
-        if step == 3:
+    def send_rows(occ):
+        for hop, far in enumerate(fars):
+            copy = remote(
+                own.at[occ], row_slot(occ, aux_place), row_send.at[occ, hop],
+                row_recv.at[occ, hop], {"aux": far * 2 + core},
+            )
+            copy.start()
+            row_copies[occ, hop] = copy
+
+    def pass_rows(occ):
+        for hop in range(len(fars)):
+            row_copies[occ, hop].wait_recv()
+            sender = lax.rem(far_place + far_count - 1 - hop, far_count) * 2 + core
+            copy = remote(
+                row_slot(occ, sender), row_slot(occ, sender), pass_send.at[occ, hop + 1],
+                pass_recv.at[occ, hop + 1], sibling,
+            )
+            copy.start()
+            pass_copies[occ, hop + 1] = copy
+
+    waves = [order[at : at + 2] for at in range(0, occs, 2)]
+    beats = virt_count - 2 + len(waves)
+    for beat in range(beats):
+        for at, wave in enumerate(waves):
+            step = beat - at
+            for occ in wave:
+                if step == 0:
+                    finish_sum(occ)
+                elif 0 < step < virt_count - 1:
+                    ring[occ, step - 1].wait_recv()
+                    ring[occ, step] = ring_copy(occ, step)
+                    ring[occ, step].start()
+        if beat == len(waves) - 1:
             for occ in order:
-                for hop in range(len(fars)):
-                    row_copies[occ, hop].wait_recv()
-                    sender = lax.rem(far_place + far_count - 1 - hop, far_count) * 2 + core
-                    copy = remote(
-                        row_slot(occ, sender), row_slot(occ, sender), pass_send.at[occ, hop + 1],
-                        pass_recv.at[occ, hop + 1], sibling,
-                    )
-                    copy.start()
-                    pass_copies[occ, hop + 1] = copy
+                send_rows(occ)
+        if beat == beats - 2:
+            for occ in order:
+                pass_rows(occ)
     for occ in order:
         ring[occ, virt_count - 2].wait_recv()
     for copy in pass_copies.values():

time: 291 us -> 282 us (0.969)
  Pallas kernels: 251 us -> 241 us
    pallas_call x1, Pallas kernels: 191 us -> 182 us  [gather_fitted(): pl.pallas_call(functools.partial(gather_kernel, aux_count, virt_count), o...]
where the time goes in v4:
time: 282 us; the launch traced here: 281 us
  Pallas kernels  241 us (85%)
  matrix products  36.4 us (13%)
  local copies, waits for them, and re-layouts  3.21 us (1%)
    pallas_call x1, Pallas kernels, gather_fitted(): pl.pallas_call(functools.partial(gather_kernel, aux_count, virt_count), o...  182 us
    pallas_call x1, Pallas kernels, scattered_density(): pl.pallas_call(functools.partial(density_kernel, aux_count), out_shape=ja...  59.1 us
    dot_general x1, matrix products, shards(): lax.dot_general(rows2, cols2, (((1,), (1,)), ((), ())), precision=precise...  22.8 us
    dot_general x1, matrix products, shards(): lax.dot_general(by_occ, metric_root, (((1,), (1,)), ((), ())), precision=...  13.6 us

profile of v4, /device:TPU:0, one launch (start us, length us, event | category | flops | bytes accessed | tf_op | source)
XLA Modules:
  0.0 281.4 jit_solution(7243041999428380057)
XLA Ops:
  0.0 0.0 copy-start
  0.0 1.5 copy-done
  1.5 13.6 %fusion.partial = f32[6,2,2,32,2560]{4,3,2,1,0:T(8,128)} fusion(f32[6,2,2,32,640]{4,3,2,1,0:T(8,128)S(1)} %bitcast.16, f32[2560,640]{1,0:T(8,128)} %param.7), kind=kOutput, calls=%fused_computation | convolution fusion | flops 7549747200 | bytes 16384000 | tf_op jit(solution)/shard_map/dot_general | solution.py:367
  15.1 181.7 %shard_map.64 = (f32[6,128,2560]{2,1,0:T(8,128)S(1)}, f32[6,256,2560]{2,1,0:T(8,128)}) custom-call(f32[6,2,2,32,2560]{4,3,2,1,0:T(8,128)} %fusion.partial), custom_call_target="tpu_custom_call" | custom-call | bytes 47185920 | tf_op jit(solution)/shard_map/pallas_call | solution.py:174
  196.9 0.0 copy-start.3
  196.9 0.0 copy-start.4
  196.9 0.0 copy-start.1
  196.9 0.0 copy-start.2
  196.9 22.8 %fusion.2.pair = f32[768,1536]{1,0:T(8,128)} fusion(f32[768,2560]{1,0:T(8,128)S(1)} %bitcast.18, f32[1536,2560]{1,0:T(8,128)} %bitcast.19), kind=kOutput, calls=%fused_computation.8 | convolution fusion | flops 18119393280 | bytes 28311552 | tf_op jit(solution)/shard_map/dot_general | solution.py:378
  219.8 0.0 copy-done.3
  219.8 0.0 copy-done.4
  219.8 0.2 select_reduce_fusion.1.occ_levels
  220.0 0.0 copy-done.1
  220.0 0.0 copy-done.2
  220.0 0.7 select_reduce_fusion
  220.6 0.1 dynamic-slice_bitcast_fusion
  220.7 0.1 copy.9.row_levels
  220.8 0.1 reshape.18
  220.9 0.1 broadcast_in_dim_reshape.3.col_levels
  221.0 59.1 %shard_map.65 = f32[6,128,640]{2,1,0:T(8,128)S(1)} custom-call(f32[768,1536]{1,0:T(8,128)} %fusion.2.pair, f32[6]{0:T(128)S(1)} %select_reduce_fusion.1.occ_levels, f32[128,1]{1,0:T(8,128)S(1)} %copy.9.row_levels, f32[1,256]{1,0:T(1,128)S(1)} %broadcast_in_dim_reshape.3.col_levels, f32[1536,2560]{1,0:T(8,128)} %bitcast.20), custom_call_target="tpu_custom_call" | custom-call | flops 18119393280 | bytes 15728640 | tf_op jit(solution)/shard_map/pallas_call | solution.py:320
  280.1 1.3 copy.12
  (1 shorter events, 0.0 us)
Async XLA Ops:
  0.0 1.5 copy-start
  196.9 22.9 %copy-start.3 = (f32[256]{0:T(256)S(1)}, f32[256]{0:T(256)}, u32[]{:S(2)}) copy-start(f32[256]{0:T(256)} %param.8) | copy-start | bytes 3076
  196.9 22.9 %copy-start.4 = (s32[6]{0:T(128)S(1)}, s32[6]{0:T(128)}, u32[]{:S(2)}) copy-start(s32[6]{0:T(128)} %param.10) | copy-start | bytes 76
  196.9 23.1 %copy-start.1 = (f32[1024]{0:T(1024)S(1)}, f32[1024]{0:T(1024)}, u32[]{:S(2)}) copy-start(f32[1024]{0:T(1024)} %param.9) | copy-start | bytes 12292
  196.9 23.1 %copy-start.2 = (s32[1024]{0:T(1024)S(1)}, s32[1024]{0:T(1024)}, u32[]{:S(2)}) copy-start(s32[1024]{0:T(1024)} %param.11) | copy-start | bytes 12292
